TPU v7x, 32 devices: a whole 2x2x4 slice. The times are simulated.
32 devices in a mesh: leaf: 16 (over z, y, x), dom: 2 (over core).
Axes of the slice: x: 2, y: 2, z: 4, core: 2. Of those that a mesh axis runs over, the one named last changes fastest.
Arguments:
- multipoles: float32 [2048, 64], P(('leaf', 'dom')), may hold values from -6 to 6
- positions: float32 [2048, 3, 256], P(('leaf', 'dom')), may hold values from 0 to 2
- charges: float32 [2048, 256], P(('leaf', 'dom')), may hold values from -6 to 6
- counts: int32 [2048], P(('leaf', 'dom')), may hold values from 1 to 256
- parents: float32 [256, 64], P('leaf', 'dom'), may hold values from -6 to 6
- parent_child_operators: float32 [8, 64, 64], replicated, may hold values from -0.75 to 0.75
- m2l: float32 [316, 64, 64], replicated, may hold values from -0.0625 to 0.0625
- m2l_list: int32 [2048, 316], P(('leaf', 'dom')), may hold values from -1 to 2047, as said below
- ulist: int32 [2048, 27], P(('leaf', 'dom')), may hold values from 0 to 2047, as said below
Outputs:
- locals_out: float32 [2048, 64], P(('leaf', 'dom'))
- near_field: float32 [2048, 256], P(('leaf', 'dom'))
Inputs may be any that keep to these rules, and one draw needn't show every extreme that they name: `m2l_list`: every entry that is not -1 lies within 256 of its row's box index; in every row a box exactly 256 away is named in the first column. `ulist`: every entry lies within 256 of its row's box index; the first column names the row's own box, the second a box exactly 256 away.
All inputs are finite; a program needn't handle non-finite values.
Results may differ from a plain program's by a relative error of at most 0.0003.
Values sent between devices are 32-bit elements; how exact they have to be, the bound alone decides.
A program may use at most 64 MiB of HBM per device.

v0:
```python
import jax
import jax.numpy as jnp
from jax import lax
from jax.sharding import PartitionSpec as P

REACH = 4


coef = 0.07957747154594767
soften = 0.0025


def shifted(array, axis, by):
    devices = lax.axis_size(axis)
    pairs = [(i, i + by) for i in range(devices) if 0 <= i + by < devices]
    return lax.ppermute(array, axis, pairs)


def widen(piece, amount):
    return shifted(piece, ("leaf", "dom"), amount)


def local(
    multipoles, positions, charges, counts, parents, parent_child_operators, m2l, m2l_list, ulist
):
    leaf_box_list = multipoles.shape[0]
    box_width = multipoles.shape[1]
    slots = charges.shape[1]
    groups = lax.axis_size("dom")
    half_id = lax.axis_index("dom")
    device = lax.axis_index("leaf") * groups + half_id
    live = jnp.arange(slots, dtype=jnp.int32)[None, :] < counts[:, None]
    live_charge = jnp.where(live, charges, jnp.zeros_like(charges))
    family = leaf_box_list // 8
    whole = lax.all_gather(parents, "dom", axis=1, tiled=True)
    owned_boxes = lax.dynamic_slice_in_dim(whole, half_id * family, family, 0)
    child_octant = jnp.einsum(
        "xky,dy->dxk", parent_child_operators, owned_boxes, precision=lax.Precision.HIGHEST
    ).reshape(leaf_box_list, box_width)
    own = (multipoles, positions, live_charge)
    lower = own
    upper = own
    held = 0
    while held < REACH:
        step = min(held + 1, REACH - held)
        low_piece = tuple((member[: step * leaf_box_list] for member in lower))
        high_piece = tuple((member[member.shape[0] - step * leaf_box_list :] for member in upper))
        got_low = widen(low_piece, step)
        got_high = widen(high_piece, -step)
        lower = tuple(
            (jnp.concatenate([fresh, member], axis=0) for fresh, member in zip(got_low, lower))
        )
        upper = tuple(
            (jnp.concatenate([member, fresh], axis=0) for fresh, member in zip(got_high, upper))
        )
        held = held + step
    extended_multipoles = jnp.concatenate([lower[0], upper[0][leaf_box_list:]], axis=0)
    ext_pos = jnp.concatenate([lower[1], upper[1][leaf_box_list:]], axis=0)
    extended_charges = jnp.concatenate([lower[2], upper[2][leaf_box_list:]], axis=0)
    base = (device - REACH) * leaf_box_list
    extent = extended_multipoles.shape[0]
    valid = m2l_list >= 0
    rows = jnp.clip(m2l_list - base, 0, extent - 1)
    picked = extended_multipoles[rows] * valid[..., None].astype(extended_multipoles.dtype)
    locals_out = child_octant + jnp.einsum(
        "bvq,vpq->bp", picked, m2l, precision=lax.Precision.HIGHEST
    )
    near_ids = jnp.clip(ulist - base, 0, extent - 1)

    def near_term(total, column_ids):
        source_pos = ext_pos[column_ids]
        source_chg = extended_charges[column_ids]
        distance = jnp.zeros((leaf_box_list, slots, slots), jnp.float32)
        for component in range(3):
            separation = positions[:, component, :, None] - source_pos[:, component, None, :]
            distance = distance + separation * separation
        kernel = coef * lax.rsqrt(distance + soften)
        return (
            total + jnp.einsum("bts,bs->bt", kernel, source_chg, precision=lax.Precision.HIGHEST),
            None,
        )

    start_total = jnp.zeros((leaf_box_list, slots), jnp.float32)
    near_field, _ = lax.scan(near_term, start_total, near_ids.T)
    return (locals_out, near_field)


def solution(mesh):
    placed = (
        P(("leaf", "dom"), None),
        P(("leaf", "dom"), None, None),
        P(("leaf", "dom"), None),
        P(("leaf", "dom")),
        P("leaf", "dom"),
        P(),
        P(),
        P(("leaf", "dom"), None),
        P(("leaf", "dom"), None),
    )
    return jax.shard_map(
        local,
        mesh=mesh,
        in_specs=placed,
        out_specs=(P(("leaf", "dom"), None), P(("leaf", "dom"), None)),
        check_vma=False,
    )
```

profile of v0, /device:TPU:20, one launch (start us, length us, event | category | flops | bytes accessed | tf_op | source)
XLA Modules:
  0.0 888.3 jit_solution(17497825835508053766)
XLA Ops:
  44.5 38.0 %gather_fusion.2 = f32[20224,64]{1,0:T(8,128)} fusion(f32[576,64]{1,0:T(8,128)S(1)} %constant_dynamic-update-slice_fusion, s32[20480]{0:T(1024)S(1)} %pad_clamp_fusion.1), kind=kCustom, calls=%fused_computation.2 | custom fusion | bytes 10435584 | tf_op jit(solution)/shard_map/gather | solution.py:64
  165.3 722.3 %while.11 = (s32[]{:T(128)}, f32[64,256]{1,0:T(8,128)S(1)}, f32[64,3,256]{2,0,1:T(8,128)S(1)}, s32[27,64]{1,0:T(8,128)S(1)}, f32[576,3,256]{2,1,0:T(4,128)}, /*index=5*/f32[576,256]{1,0:T(8,128)S(1)}, s32[]{:T(128)}, s32[]{:T(128)}) while((s32[]{:T(128)}, f32[64,256]{1,0:T(8,128)S(1)}, f32[64,3,256]{2,0,1:T(8,128)S(1)}, ...), condition=%wide.region_1.2_spmd.clone, body=%wide.region_0.1_spmd.clone.sunk | while | flops 92308672 | bytes 2430315 | solution.py:84
  168.6 23.4 %fusion.54 = f32[64,1,256]{2,1,0:T(1,128)S(1)} fusion(f32[64,256]{1,0:T(8,128)S(1)} %get-tuple-element.131, f32[64,256]{1,0:T(8,128)S(1)} %get-tuple-element.133, f32[64,256]{1,0:T(8,128)S(1)} %get-tuple-element.134, f32[64,256]{1,0:T(8,128)S(1)} %get-tuple-element.135, f32[64,256]{1,0:T(8,128)S(1)} %get-tuple-element.136, ...), kind=kOutput, calls=%fused_computation.3.clone.1 | convolution fusion | flops 92274688 | bytes 524288 | tf_op jit(solution)/shard_map/while/body/eval_jaxpr/bts,bs->bt/dot_general | solution.py:79
  195.3 23.4 %fusion.54 = f32[64,1,256]{2,1,0:T(1,128)S(1)} fusion(f32[64,256]{1,0:T(8,128)S(1)} %get-tuple-element.131, f32[64,256]{1,0:T(8,128)S(1)} %get-tuple-element.133, f32[64,256]{1,0:T(8,128)S(1)} %get-tuple-element.134, f32[64,256]{1,0:T(8,128)S(1)} %get-tuple-element.135, f32[64,256]{1,0:T(8,128)S(1)} %get-tuple-element.136, ...), kind=kOutput, calls=%fused_computation.3.clone.1 | convolution fusion | flops 92274688 | bytes 524288 | tf_op jit(solution)/shard_map/while/body/eval_jaxpr/bts,bs->bt/dot_general | solution.py:79
  222.1 23.4 %fusion.54 = f32[64,1,256]{2,1,0:T(1,128)S(1)} fusion(f32[64,256]{1,0:T(8,128)S(1)} %get-tuple-element.131, f32[64,256]{1,0:T(8,128)S(1)} %get-tuple-element.133, f32[64,256]{1,0:T(8,128)S(1)} %get-tuple-element.134, f32[64,256]{1,0:T(8,128)S(1)} %get-tuple-element.135, f32[64,256]{1,0:T(8,128)S(1)} %get-tuple-element.136, ...), kind=kOutput, calls=%fused_computation.3.clone.1 | convolution fusion | flops 92274688 | bytes 524288 | tf_op jit(solution)/shard_map/while/body/eval_jaxpr/bts,bs->bt/dot_general | solution.py:79
  248.8 23.4 %fusion.54 = f32[64,1,256]{2,1,0:T(1,128)S(1)} fusion(f32[64,256]{1,0:T(8,128)S(1)} %get-tuple-element.131, f32[64,256]{1,0:T(8,128)S(1)} %get-tuple-element.133, f32[64,256]{1,0:T(8,128)S(1)} %get-tuple-element.134, f32[64,256]{1,0:T(8,128)S(1)} %get-tuple-element.135, f32[64,256]{1,0:T(8,128)S(1)} %get-tuple-element.136, ...), kind=kOutput, calls=%fused_computation.3.clone.1 | convolution fusion | flops 92274688 | bytes 524288 | tf_op jit(solution)/shard_map/while/body/eval_jaxpr/bts,bs->bt/dot_general | solution.py:79
  275.6 23.4 %fusion.54 = f32[64,1,256]{2,1,0:T(1,128)S(1)} fusion(f32[64,256]{1,0:T(8,128)S(1)} %get-tuple-element.131, f32[64,256]{1,0:T(8,128)S(1)} %get-tuple-element.133, f32[64,256]{1,0:T(8,128)S(1)} %get-tuple-element.134, f32[64,256]{1,0:T(8,128)S(1)} %get-tuple-element.135, f32[64,256]{1,0:T(8,128)S(1)} %get-tuple-element.136, ...), kind=kOutput, calls=%fused_computation.3.clone.1 | convolution fusion | flops 92274688 | bytes 524288 | tf_op jit(solution)/shard_map/while/body/eval_jaxpr/bts,bs->bt/dot_general | solution.py:79
  302.4 23.4 %fusion.54 = f32[64,1,256]{2,1,0:T(1,128)S(1)} fusion(f32[64,256]{1,0:T(8,128)S(1)} %get-tuple-element.131, f32[64,256]{1,0:T(8,128)S(1)} %get-tuple-element.133, f32[64,256]{1,0:T(8,128)S(1)} %get-tuple-element.134, f32[64,256]{1,0:T(8,128)S(1)} %get-tuple-element.135, f32[64,256]{1,0:T(8,128)S(1)} %get-tuple-element.136, ...), kind=kOutput, calls=%fused_computation.3.clone.1 | convolution fusion | flops 92274688 | bytes 524288 | tf_op jit(solution)/shard_map/while/body/eval_jaxpr/bts,bs->bt/dot_general | solution.py:79
  329.1 23.4 %fusion.54 = f32[64,1,256]{2,1,0:T(1,128)S(1)} fusion(f32[64,256]{1,0:T(8,128)S(1)} %get-tuple-element.131, f32[64,256]{1,0:T(8,128)S(1)} %get-tuple-element.133, f32[64,256]{1,0:T(8,128)S(1)} %get-tuple-element.134, f32[64,256]{1,0:T(8,128)S(1)} %get-tuple-element.135, f32[64,256]{1,0:T(8,128)S(1)} %get-tuple-element.136, ...), kind=kOutput, calls=%fused_computation.3.clone.1 | convolution fusion | flops 92274688 | bytes 524288 | tf_op jit(solution)/shard_map/while/body/eval_jaxpr/bts,bs->bt/dot_general | solution.py:79
  355.9 23.4 %fusion.54 = f32[64,1,256]{2,1,0:T(1,128)S(1)} fusion(f32[64,256]{1,0:T(8,128)S(1)} %get-tuple-element.131, f32[64,256]{1,0:T(8,128)S(1)} %get-tuple-element.133, f32[64,256]{1,0:T(8,128)S(1)} %get-tuple-element.134, f32[64,256]{1,0:T(8,128)S(1)} %get-tuple-element.135, f32[64,256]{1,0:T(8,128)S(1)} %get-tuple-element.136, ...), kind=kOutput, calls=%fused_computation.3.clone.1 | convolution fusion | flops 92274688 | bytes 524288 | tf_op jit(solution)/shard_map/while/body/eval_jaxpr/bts,bs->bt/dot_general | solution.py:79
  382.6 23.4 %fusion.54 = f32[64,1,256]{2,1,0:T(1,128)S(1)} fusion(f32[64,256]{1,0:T(8,128)S(1)} %get-tuple-element.131, f32[64,256]{1,0:T(8,128)S(1)} %get-tuple-element.133, f32[64,256]{1,0:T(8,128)S(1)} %get-tuple-element.134, f32[64,256]{1,0:T(8,128)S(1)} %get-tuple-element.135, f32[64,256]{1,0:T(8,128)S(1)} %get-tuple-element.136, ...), kind=kOutput, calls=%fused_computation.3.clone.1 | convolution fusion | flops 92274688 | bytes 524288 | tf_op jit(solution)/shard_map/while/body/eval_jaxpr/bts,bs->bt/dot_general | solution.py:79
  409.4 23.4 %fusion.54 = f32[64,1,256]{2,1,0:T(1,128)S(1)} fusion(f32[64,256]{1,0:T(8,128)S(1)} %get-tuple-element.131, f32[64,256]{1,0:T(8,128)S(1)} %get-tuple-element.133, f32[64,256]{1,0:T(8,128)S(1)} %get-tuple-element.134, f32[64,256]{1,0:T(8,128)S(1)} %get-tuple-element.135, f32[64,256]{1,0:T(8,128)S(1)} %get-tuple-element.136, ...), kind=kOutput, calls=%fused_computation.3.clone.1 | convolution fusion | flops 92274688 | bytes 524288 | tf_op jit(solution)/shard_map/while/body/eval_jaxpr/bts,bs->bt/dot_general | solution.py:79
  436.1 23.4 %fusion.54 = f32[64,1,256]{2,1,0:T(1,128)S(1)} fusion(f32[64,256]{1,0:T(8,128)S(1)} %get-tuple-element.131, f32[64,256]{1,0:T(8,128)S(1)} %get-tuple-element.133, f32[64,256]{1,0:T(8,128)S(1)} %get-tuple-element.134, f32[64,256]{1,0:T(8,128)S(1)} %get-tuple-element.135, f32[64,256]{1,0:T(8,128)S(1)} %get-tuple-element.136, ...), kind=kOutput, calls=%fused_computation.3.clone.1 | convolution fusion | flops 92274688 | bytes 524288 | tf_op jit(solution)/shard_map/while/body/eval_jaxpr/bts,bs->bt/dot_general | solution.py:79
  462.9 23.4 %fusion.54 = f32[64,1,256]{2,1,0:T(1,128)S(1)} fusion(f32[64,256]{1,0:T(8,128)S(1)} %get-tuple-element.131, f32[64,256]{1,0:T(8,128)S(1)} %get-tuple-element.133, f32[64,256]{1,0:T(8,128)S(1)} %get-tuple-element.134, f32[64,256]{1,0:T(8,128)S(1)} %get-tuple-element.135, f32[64,256]{1,0:T(8,128)S(1)} %get-tuple-element.136, ...), kind=kOutput, calls=%fused_computation.3.clone.1 | convolution fusion | flops 92274688 | bytes 524288 | tf_op jit(solution)/shard_map/while/body/eval_jaxpr/bts,bs->bt/dot_general | solution.py:79
  489.6 23.4 %fusion.54 = f32[64,1,256]{2,1,0:T(1,128)S(1)} fusion(f32[64,256]{1,0:T(8,128)S(1)} %get-tuple-element.131, f32[64,256]{1,0:T(8,128)S(1)} %get-tuple-element.133, f32[64,256]{1,0:T(8,128)S(1)} %get-tuple-element.134, f32[64,256]{1,0:T(8,128)S(1)} %get-tuple-element.135, f32[64,256]{1,0:T(8,128)S(1)} %get-tuple-element.136, ...), kind=kOutput, calls=%fused_computation.3.clone.1 | convolution fusion | flops 92274688 | bytes 524288 | tf_op jit(solution)/shard_map/while/body/eval_jaxpr/bts,bs->bt/dot_general | solution.py:79
  516.4 23.4 %fusion.54 = f32[64,1,256]{2,1,0:T(1,128)S(1)} fusion(f32[64,256]{1,0:T(8,128)S(1)} %get-tuple-element.131, f32[64,256]{1,0:T(8,128)S(1)} %get-tuple-element.133, f32[64,256]{1,0:T(8,128)S(1)} %get-tuple-element.134, f32[64,256]{1,0:T(8,128)S(1)} %get-tuple-element.135, f32[64,256]{1,0:T(8,128)S(1)} %get-tuple-element.136, ...), kind=kOutput, calls=%fused_computation.3.clone.1 | convolution fusion | flops 92274688 | bytes 524288 | tf_op jit(solution)/shard_map/while/body/eval_jaxpr/bts,bs->bt/dot_general | solution.py:79
  543.1 23.4 %fusion.54 = f32[64,1,256]{2,1,0:T(1,128)S(1)} fusion(f32[64,256]{1,0:T(8,128)S(1)} %get-tuple-element.131, f32[64,256]{1,0:T(8,128)S(1)} %get-tuple-element.133, f32[64,256]{1,0:T(8,128)S(1)} %get-tuple-element.134, f32[64,256]{1,0:T(8,128)S(1)} %get-tuple-element.135, f32[64,256]{1,0:T(8,128)S(1)} %get-tuple-element.136, ...), kind=kOutput, calls=%fused_computation.3.clone.1 | convolution fusion | flops 92274688 | bytes 524288 | tf_op jit(solution)/shard_map/while/body/eval_jaxpr/bts,bs->bt/dot_general | solution.py:79
  569.9 23.4 %fusion.54 = f32[64,1,256]{2,1,0:T(1,128)S(1)} fusion(f32[64,256]{1,0:T(8,128)S(1)} %get-tuple-element.131, f32[64,256]{1,0:T(8,128)S(1)} %get-tuple-element.133, f32[64,256]{1,0:T(8,128)S(1)} %get-tuple-element.134, f32[64,256]{1,0:T(8,128)S(1)} %get-tuple-element.135, f32[64,256]{1,0:T(8,128)S(1)} %get-tuple-element.136, ...), kind=kOutput, calls=%fused_computation.3.clone.1 | convolution fusion | flops 92274688 | bytes 524288 | tf_op jit(solution)/shard_map/while/body/eval_jaxpr/bts,bs->bt/dot_general | solution.py:79
  596.6 23.4 %fusion.54 = f32[64,1,256]{2,1,0:T(1,128)S(1)} fusion(f32[64,256]{1,0:T(8,128)S(1)} %get-tuple-element.131, f32[64,256]{1,0:T(8,128)S(1)} %get-tuple-element.133, f32[64,256]{1,0:T(8,128)S(1)} %get-tuple-element.134, f32[64,256]{1,0:T(8,128)S(1)} %get-tuple-element.135, f32[64,256]{1,0:T(8,128)S(1)} %get-tuple-element.136, ...), kind=kOutput, calls=%fused_computation.3.clone.1 | convolution fusion | flops 92274688 | bytes 524288 | tf_op jit(solution)/shard_map/while/body/eval_jaxpr/bts,bs->bt/dot_general | solution.py:79
  623.4 23.4 %fusion.54 = f32[64,1,256]{2,1,0:T(1,128)S(1)} fusion(f32[64,256]{1,0:T(8,128)S(1)} %get-tuple-element.131, f32[64,256]{1,0:T(8,128)S(1)} %get-tuple-element.133, f32[64,256]{1,0:T(8,128)S(1)} %get-tuple-element.134, f32[64,256]{1,0:T(8,128)S(1)} %get-tuple-element.135, f32[64,256]{1,0:T(8,128)S(1)} %get-tuple-element.136, ...), kind=kOutput, calls=%fused_computation.3.clone.1 | convolution fusion | flops 92274688 | bytes 524288 | tf_op jit(solution)/shard_map/while/body/eval_jaxpr/bts,bs->bt/dot_general | solution.py:79
  650.1 23.4 %fusion.54 = f32[64,1,256]{2,1,0:T(1,128)S(1)} fusion(f32[64,256]{1,0:T(8,128)S(1)} %get-tuple-element.131, f32[64,256]{1,0:T(8,128)S(1)} %get-tuple-element.133, f32[64,256]{1,0:T(8,128)S(1)} %get-tuple-element.134, f32[64,256]{1,0:T(8,128)S(1)} %get-tuple-element.135, f32[64,256]{1,0:T(8,128)S(1)} %get-tuple-element.136, ...), kind=kOutput, calls=%fused_computation.3.clone.1 | convolution fusion | flops 92274688 | bytes 524288 | tf_op jit(solution)/shard_map/while/body/eval_jaxpr/bts,bs->bt/dot_general | solution.py:79
  676.9 23.4 %fusion.54 = f32[64,1,256]{2,1,0:T(1,128)S(1)} fusion(f32[64,256]{1,0:T(8,128)S(1)} %get-tuple-element.131, f32[64,256]{1,0:T(8,128)S(1)} %get-tuple-element.133, f32[64,256]{1,0:T(8,128)S(1)} %get-tuple-element.134, f32[64,256]{1,0:T(8,128)S(1)} %get-tuple-element.135, f32[64,256]{1,0:T(8,128)S(1)} %get-tuple-element.136, ...), kind=kOutput, calls=%fused_computation.3.clone.1 | convolution fusion | flops 92274688 | bytes 524288 | tf_op jit(solution)/shard_map/while/body/eval_jaxpr/bts,bs->bt/dot_general | solution.py:79
  703.6 23.4 %fusion.54 = f32[64,1,256]{2,1,0:T(1,128)S(1)} fusion(f32[64,256]{1,0:T(8,128)S(1)} %get-tuple-element.131, f32[64,256]{1,0:T(8,128)S(1)} %get-tuple-element.133, f32[64,256]{1,0:T(8,128)S(1)} %get-tuple-element.134, f32[64,256]{1,0:T(8,128)S(1)} %get-tuple-element.135, f32[64,256]{1,0:T(8,128)S(1)} %get-tuple-element.136, ...), kind=kOutput, calls=%fused_computation.3.clone.1 | convolution fusion | flops 92274688 | bytes 524288 | tf_op jit(solution)/shard_map/while/body/eval_jaxpr/bts,bs->bt/dot_general | solution.py:79
  757.2 23.4 %fusion.54 = f32[64,1,256]{2,1,0:T(1,128)S(1)} fusion(f32[64,256]{1,0:T(8,128)S(1)} %get-tuple-element.131, f32[64,256]{1,0:T(8,128)S(1)} %get-tuple-element.133, f32[64,256]{1,0:T(8,128)S(1)} %get-tuple-element.134, f32[64,256]{1,0:T(8,128)S(1)} %get-tuple-element.135, f32[64,256]{1,0:T(8,128)S(1)} %get-tuple-element.136, ...), kind=kOutput, calls=%fused_computation.3.clone.1 | convolution fusion | flops 92274688 | bytes 524288 | tf_op jit(solution)/shard_map/while/body/eval_jaxpr/bts,bs->bt/dot_general | solution.py:79
  (314 shorter events, 331.4 us)
Async XLA Ops:
  0.6 21.1 %copy-start = (f32[8,64,64]{2,1,0:T(8,128)S(1)}, f32[8,64,64]{2,1,0:T(8,128)}, u32[]{:S(2)}) copy-start(f32[8,64,64]{2,1,0:T(8,128)} %param.16) | copy-start | bytes 393220
  0.6 21.8 %collective-permute-start.3 = (f32[64,64]{1,0:T(8,128)}, f32[64,64]{1,0:T(8,128)S(1)}, u32[]{:S(2)}, u32[]{:S(2)}) collective-permute-start(f32[64,64]{1,0:T(8,128)} %param.11), channel_id=1, source_target_pairs={{1,0},{2,1},{3,2},{4,3},{5,4},{6,5},{7,6},{8,7},{9,8},{10,9},{11,1... | collective-permute-start | bytes 49160 | tf_op jit(solution)/shard_map/ppermute | solution.py:16
  3.6 18.9 %collective-permute-start = (f32[64,64]{1,0:T(8,128)}, f32[64,64]{1,0:T(8,128)S(1)}, u32[]{:S(2)}, u32[]{:S(2)}) collective-permute-start(f32[64,64]{1,0:T(8,128)} %param.11), channel_id=1, source_target_pairs={{0,1},{1,2},{2,3},{3,4},{4,5},{5,6},{6,7},{7,8},{8,9},{9,10},{10,1... | collective-permute-start | bytes 49160 | tf_op jit(solution)/shard_map/ppermute | solution.py:16
  6.6 121.9 %collective-permute-start.9 = (f32[64,3,256]{2,1,0:T(4,128)S(1)}, f32[64,3,256]{2,1,0:T(4,128)S(1)}, u32[]{:S(2)}, u32[]{:S(2)}) collective-permute-start(f32[64,3,256]{2,1,0:T(4,128)S(1)} %copy.32), channel_id=1, source_target_pairs={{1,0},{2,1},{3,2},{4,3},{5,4},{6,5},{7,6},{8,7},{9,8},{10,9},{11,1... | collective-permute-start | bytes 589832 | tf_op jit(solution)/shard_map/ppermute | solution.py:16
  11.1 117.4 %collective-permute-start.6 = (f32[64,3,256]{2,1,0:T(4,128)S(1)}, f32[64,3,256]{2,1,0:T(4,128)S(1)}, u32[]{:S(2)}, u32[]{:S(2)}) collective-permute-start(f32[64,3,256]{2,1,0:T(4,128)S(1)} %copy.32), channel_id=1, source_target_pairs={{0,1},{1,2},{2,3},{3,4},{4,5},{5,6},{6,7},{7,8},{8,9},{9,10},{10,1... | collective-permute-start | bytes 589832 | tf_op jit(solution)/shard_map/ppermute | solution.py:16
  14.0 87.2 %collective-permute-start.15 = (f32[64,256]{1,0:T(8,128)S(1)}, f32[64,256]{1,0:T(8,128)S(1)}, u32[]{:S(2)}, u32[]{:S(2)}) collective-permute-start(f32[64,256]{1,0:T(8,128)S(1)} %fusion.38), channel_id=1, source_target_pairs={{1,0},{2,1},{3,2},{4,3},{5,4},{6,5},{7,6},{8,7},{9,8},{10,9},{11,1... | collective-permute-start | bytes 196616 | tf_op jit(solution)/shard_map/ppermute | solution.py:16
  23.3 7.7 collective-permute-start.1
  28.1 7.9 collective-permute-start.4
  31.0 7.5 collective-permute-start.2
  36.0 65.2 %collective-permute-start.12 = (f32[64,256]{1,0:T(8,128)S(1)}, f32[64,256]{1,0:T(8,128)S(1)}, u32[]{:S(2)}, u32[]{:S(2)}) collective-permute-start(f32[64,256]{1,0:T(8,128)S(1)} %fusion.38), channel_id=1, source_target_pairs={{0,1},{1,2},{2,3},{3,4},{4,5},{5,6},{6,7},{7,8},{8,9},{9,10},{10,1... | collective-permute-start | bytes 196616 | tf_op jit(solution)/shard_map/ppermute | solution.py:16
  38.5 6.1 collective-permute-start.5
  101.2 20.6 %collective-permute-start.13 = (f32[128,256]{1,0:T(8,128)S(1)}, f32[128,256]{1,0:T(8,128)S(1)}, u32[]{:S(2)}, u32[]{:S(2)}) collective-permute-start(f32[128,256]{1,0:T(8,128)S(1)} %get-tuple-element.80), channel_id=1, source_target_pairs={{0,2},{1,3},{2,4},{3,5},{4,6},{5,7},{6,8},{7,9},{8,10},{9,11},{10,... | collective-permute-start | bytes 393224 | tf_op jit(solution)/shard_map/ppermute | solution.py:16
  105.6 29.9 %copy-start.4 = (f32[64,256]{1,0:T(8,128)S(1)}, f32[64,256]{1,0:T(8,128)}, u32[]{:S(2)}) copy-start(f32[64,256]{1,0:T(8,128)} %param.13) | copy-start | bytes 196612
  105.7 29.9 %copy-start.5 = (s32[64]{0:T(128)S(1)}, s32[64]{0:T(128)}, u32[]{:S(2)}) copy-start(s32[64]{0:T(128)} %param.14) | copy-start | bytes 772
  105.7 20.3 %collective-permute-start.16 = (f32[128,256]{1,0:T(8,128)S(1)}, f32[128,256]{1,0:T(8,128)S(1)}, u32[]{:S(2)}, u32[]{:S(2)}) collective-permute-start(f32[128,256]{1,0:T(8,128)S(1)} %get-tuple-element.79), channel_id=1, source_target_pairs={{2,0},{3,1},{4,2},{5,3},{6,4},{7,5},{8,6},{9,7},{10,8},{11,9},{12,... | collective-permute-start | bytes 393224 | tf_op jit(solution)/shard_map/ppermute | solution.py:16
  121.8 38.6 %copy-start.1 = (f32[64,3,256]{2,0,1:T(8,128)S(1)}, f32[64,3,256]{2,0,1:T(8,128)}, u32[]{:S(2)}) copy-start(f32[64,3,256]{2,0,1:T(8,128)} %param.12) | copy-start | bytes 589828
  121.8 13.6 %collective-permute-start.14 = (f32[64,256]{1,0:T(8,128)S(1)}, f32[64,256]{1,0:T(8,128)S(1)}, u32[]{:S(2)}, u32[]{:S(2)}) collective-permute-start(f32[64,256]{1,0:T(8,128)S(1)} %slice.67), channel_id=1, source_target_pairs={{0,1},{1,2},{2,3},{3,4},{4,5},{5,6},{6,7},{7,8},{8,9},{9,10},{10,1... | collective-permute-start | bytes 196616 | tf_op jit(solution)/shard_map/ppermute | solution.py:16
  126.0 22.3 %collective-permute-start.17 = (f32[64,256]{1,0:T(8,128)S(1)}, f32[64,256]{1,0:T(8,128)S(1)}, u32[]{:S(2)}, u32[]{:S(2)}) collective-permute-start(f32[64,256]{1,0:T(8,128)S(1)} %slice.68), channel_id=1, source_target_pairs={{1,0},{2,1},{3,2},{4,3},{5,4},{6,5},{7,6},{8,7},{9,8},{10,9},{11,1... | collective-permute-start | bytes 196616 | tf_op jit(solution)/shard_map/ppermute | solution.py:16
  128.7 17.6 %collective-permute-start.7 = (f32[128,3,256]{2,1,0:T(4,128)S(1)}, f32[128,3,256]{2,1,0:T(4,128)S(1)}, u32[]{:S(2)}, u32[]{:S(2)}) collective-permute-start(f32[128,3,256]{2,1,0:T(4,128)S(1)} %get-tuple-element.78), channel_id=1, source_target_pairs={{0,2},{1,3},{2,4},{3,5},{4,6},{5,7},{6,8},{7,9},{8,10},{9,11},{10,... | collective-permute-start | bytes 1179656 | tf_op jit(solution)/shard_map/ppermute | solution.py:16
  131.7 25.3 %collective-permute-start.10 = (f32[128,3,256]{2,1,0:T(4,128)S(1)}, f32[128,3,256]{2,1,0:T(4,128)S(1)}, u32[]{:S(2)}, u32[]{:S(2)}) collective-permute-start(f32[128,3,256]{2,1,0:T(4,128)S(1)} %get-tuple-element.77), channel_id=1, source_target_pairs={{2,0},{3,1},{4,2},{5,3},{6,4},{7,5},{8,6},{9,7},{10,8},{11,9},{12,... | collective-permute-start | bytes 1179656 | tf_op jit(solution)/shard_map/ppermute | solution.py:16
  146.3 13.8 %collective-permute-start.8 = (f32[64,3,256]{2,1,0:T(4,128)S(1)}, f32[64,3,256]{2,1,0:T(4,128)S(1)}, u32[]{:S(2)}, u32[]{:S(2)}) collective-permute-start(f32[64,3,256]{2,1,0:T(4,128)S(1)} %slice.65), channel_id=1, source_target_pairs={{0,1},{1,2},{2,3},{3,4},{4,5},{5,6},{6,7},{7,8},{8,9},{9,10},{10,1... | collective-permute-start | bytes 589832 | tf_op jit(solution)/shard_map/ppermute | solution.py:16
  157.0 6.8 collective-permute-start.11
  163.9 1.4 copy-start.3
  887.6 0.6 copy-start.2
where the time goes:
time: 894 us; the launch traced here: 888 us
  matrix products  647 us (72%)
  local copies, waits for them, and re-layouts  148 us (17%)
  starting transfers between devices  56.2 us (6%)
  waiting for transfers between devices  26 us (3%)
    dot_general x27, matrix products, near_term(): jnp.einsum('bts,bs->bt', kernel, source_chg, precision=lax.Precision.HIGH...  633 us
    gather x27, local copies, waits for them, and re-layouts, near_term(): source_pos = ext_pos[column_ids]  64.4 us
    gather x3, local copies, waits for them, and re-layouts, local(): extended_multipoles[rows]  56.6 us
    ppermute x18, starting transfers between devices, shifted(): return lax.ppermute(array, axis, pairs)  56.2 us
    ppermute x18, waiting for transfers between devices, shifted(): return lax.ppermute(array, axis, pairs)  26 us
  transfers between devices with their start and end apart: 18, of which 5 were waited for; matrix products, arithmetic and copies ran while one was open for 9% of the time, Pallas kernels for 0%

commit v1 on v0

v1 whole, which is shorter than its diff:
```python
import functools

import jax
import jax.numpy as jnp
from jax import lax
from jax.experimental import pallas as pl
from jax.experimental.pallas import tpu as pltpu
from jax.sharding import PartitionSpec as P

REACH = 4
LANES = 128
CHUNK = 512


coef = 0.07957747154594767
soften = 0.0025


def split3(value):
    first = value.astype(jnp.bfloat16)
    rest = value - first.astype(jnp.float32)
    second = rest.astype(jnp.bfloat16)
    third = (rest - second.astype(jnp.float32)).astype(jnp.bfloat16)
    return first, second, third


def near_kernel(ku, slots, own_first, ids_ref, cnt_ref, feat_ref, out_ref, buf, tgt, acc):
    b = pl.program_id(0)
    blocks = slots // LANES
    per_chunk = CHUNK // LANES
    lane = lax.broadcasted_iota(jnp.int32, (8, LANES), 1)
    row = lax.broadcasted_iota(jnp.int32, (8, LANES), 0)
    blank = jnp.where(row == 4, 1.0, 0.0).astype(jnp.float32)

    own = feat_ref[own_first + b]
    wide_row = lax.broadcasted_iota(jnp.int32, (8, slots), 0)
    norm = jnp.broadcast_to(own[3:4, :], (8, slots)) + soften
    g = jnp.where(wide_row < 3, -2.0 * own, 0.0)
    g = jnp.where(wide_row == 3, 1.0, g)
    g = jnp.where(wide_row == 4, norm, g)
    g1, g2, g3 = (part.astype(jnp.float32) for part in split3(g))
    stacked = jnp.concatenate([g1, g1, g2, g2, g1, g3], axis=0)
    stacked = jnp.concatenate([stacked, jnp.zeros((LANES - 48, slots), jnp.float32)], axis=0)
    tgt[...] = stacked.T.astype(jnp.bfloat16)

    offset = jnp.int32(0)
    current = blank
    for k in range(ku):
        box = ids_ref[b * ku + k]
        live = cnt_ref[box]
        block = offset // LANES
        shift = offset % LANES
        keep = lane < shift
        rolled = [
            pltpu.roll(feat_ref[box, :, i * LANES : (i + 1) * LANES], shift, 1)
            for i in range(blocks)
        ]
        outs = [jnp.where(keep, current, rolled[0])]
        for i in range(1, blocks):
            outs.append(jnp.where(keep, rolled[i - 1], rolled[i]))
        outs.append(jnp.where(keep, rolled[-1], blank))
        for i, piece in enumerate(outs):
            buf[block + i] = piece
        offset = offset + live
        moved = offset // LANES - block
        current = outs[0]
        for i in range(1, blocks + 1):
            current = jnp.where(moved == i, outs[i], current)
    last = offset // LANES
    buf[last] = jnp.where(lane < offset % LANES, current, blank)
    for i in range(1, per_chunk):
        buf[last + i] = blank

    acc[...] = jnp.zeros_like(acc)

    def chunk_step(c, carry):
        feat = jnp.concatenate([buf[c * per_chunk + i] for i in range(per_chunk)], axis=1)
        f1, f2, f3 = (part.astype(jnp.float32) for part in split3(feat))
        source = jnp.concatenate(
            [f1, f2, f1, f2, f3, f1, jnp.zeros((LANES - 48, CHUNK), jnp.float32)], axis=0
        ).astype(jnp.bfloat16)
        dist = jnp.dot(tgt[...], source, preferred_element_type=jnp.float32)
        term = lax.rsqrt(dist) * feat[5:6, :]
        total = term[:, :LANES]
        for i in range(1, per_chunk):
            total = total + term[:, i * LANES : (i + 1) * LANES]
        acc[...] += total
        return carry

    chunks = (offset + CHUNK - 1) // CHUNK
    lax.fori_loop(0, chunks, chunk_step, 0)
    out_ref[0] = coef * jnp.sum(acc[...].T, axis=0, keepdims=True)


def near_call(ids, cnt, feat, boxes, own_first):
    slots = feat.shape[2]
    ku = ids.shape[0] // boxes
    room = (ku * slots + CHUNK) // LANES + slots // LANES + 2
    return pl.pallas_call(
        functools.partial(near_kernel, ku, slots, own_first),
        out_shape=jax.ShapeDtypeStruct((boxes, 1, slots), jnp.float32),
        grid_spec=pltpu.PrefetchScalarGridSpec(
            num_scalar_prefetch=2,
            grid=(boxes,),
            in_specs=[pl.BlockSpec(memory_space=pltpu.VMEM)],
            out_specs=pl.BlockSpec((1, 1, slots), lambda b, *_: (b, 0, 0)),
            scratch_shapes=[
                pltpu.VMEM((room, 8, LANES), jnp.float32),
                pltpu.VMEM((slots, LANES), jnp.bfloat16),
                pltpu.VMEM((slots, LANES), jnp.float32),
            ],
        ),
        compiler_params=pltpu.CompilerParams(vmem_limit_bytes=32 * 2**20),
    )(ids, cnt, feat)


def shifted(array, by):
    axis = ("leaf", "dom")
    devices = lax.axis_size(axis)
    pairs = [(i, i + by) for i in range(devices) if 0 <= i + by < devices]
    return lax.ppermute(array, axis, pairs)


def local(
    multipoles, positions, charges, counts, parents, parent_child_operators, m2l, m2l_list, ulist
):
    boxes = multipoles.shape[0]
    width = multipoles.shape[1]
    slots = charges.shape[1]
    groups = lax.axis_size("dom")
    half_id = lax.axis_index("dom")
    device = lax.axis_index("leaf") * groups + half_id
    live = jnp.arange(slots, dtype=jnp.int32)[None, :] < counts[:, None]
    live_charge = jnp.where(live, charges, jnp.zeros_like(charges))
    rest = jnp.concatenate(
        [
            multipoles,
            counts[:, None].astype(jnp.float32),
            jnp.zeros((boxes, slots - width - 1), jnp.float32),
        ],
        axis=1,
    )
    centred = jnp.transpose(positions, (1, 0, 2)) - 1.0
    packed = jnp.concatenate([centred, live_charge[None], rest[None]], axis=0)
    pieces = [packed if k == 0 else shifted(packed, -k) for k in range(-REACH, REACH + 1)]
    ext = jnp.concatenate(pieces, axis=1)

    family = boxes // 8
    whole = lax.all_gather(parents, "dom", axis=1, tiled=True)
    owned_boxes = lax.dynamic_slice_in_dim(whole, half_id * family, family, 0)
    child_octant = jnp.einsum(
        "xky,dy->dxk", parent_child_operators, owned_boxes, precision=lax.Precision.HIGHEST
    ).reshape(boxes, width)

    base = (device - REACH) * boxes
    extent = ext.shape[1]

    coords = ext[:3]
    norm = jnp.sum(coords * coords, axis=0)
    one = jnp.ones_like(norm)
    zero = jnp.zeros_like(norm)
    feat = jnp.stack([ext[0], ext[1], ext[2], norm, one, ext[3], zero, zero], axis=1)
    cnt = ext[4, :, width].astype(jnp.int32)
    near_ids = jnp.clip(ulist - base, 0, extent - 1).reshape(-1)
    near_field = near_call(near_ids, cnt, feat, boxes, REACH * boxes).reshape(boxes, slots)

    extended_multipoles = ext[4, :, :width]
    valid = m2l_list >= 0
    rows = jnp.clip(m2l_list - base, 0, extent - 1)
    picked = extended_multipoles[rows] * valid[..., None].astype(extended_multipoles.dtype)
    locals_out = child_octant + jnp.einsum(
        "bvq,vpq->bp", picked, m2l, precision=lax.Precision.HIGHEST
    )
    return (locals_out, near_field)


def solution(mesh):
    placed = (
        P(("leaf", "dom"), None),
        P(("leaf", "dom"), None, None),
        P(("leaf", "dom"), None),
        P(("leaf", "dom")),
        P("leaf", "dom"),
        P(),
        P(),
        P(("leaf", "dom"), None),
        P(("leaf", "dom"), None),
    )
    return jax.shard_map(
        local,
        mesh=mesh,
        in_specs=placed,
        out_specs=(P(("leaf", "dom"), None), P(("leaf", "dom"), None)),
        check_vma=False,
    )
```

time: 894 us -> 334 us (0.37)
  matrix products: 647 us -> 14.4 us
  Pallas kernels: 0 us -> 142 us
  local copies, waits for them, and re-layouts: 148 us -> 79.2 us
  starting transfers between devices: 56.2 us -> 21.6 us
  waiting for transfers between devices: 26 us -> 48 us
  other arithmetic: 5.48 us -> 20.5 us
    dot_general x27 -> x0, matrix products: 633 us -> none  [near_term(): jnp.einsum('bts,bs->bt', kernel, source_chg, precision=lax.Precision.HIGH...]
    pallas_call x0 -> x1, Pallas kernels: none -> 142 us  [near_call(): pl.pallas_call(functools.partial(near_kernel, ku, slots, own_first), out_...]
    gather x54 -> x0, local copies, waits for them, and re-layouts: 82.1 us -> none  [the longest x27 64.4 us: near_term(): source_pos = ext_pos[column_ids]]
    ppermute x18 -> x8, starting transfers between devices: 56.2 us -> 21.6 us  [shifted(): return lax.ppermute(array, axis, pairs)]
    ppermute x18 -> x8, waiting for transfers between devices: 26 us -> 48 us  [shifted(): return lax.ppermute(array, axis, pairs)]
    another operation x0 -> x5, local copies, waits for them, and re-layouts: none -> 17.2 us  [local(): jnp.stack([ext[0], ext[1], ext[2], norm, one, ext[3], zero, zero], axis=1)]
    convert_element_type x0 -> x2, other arithmetic: none -> 11.8 us  [the longest x1 11.2 us: local(): cnt = ext[4, :, width].astype(jnp.int32)]
  transfers between devices with their start and end apart: 18 -> 8, of which waited for: 5 -> 5; matrix products, arithmetic and copies ran while one was open for 9% -> 2% of each run, Pallas kernels for 0% -> 0%
where the time goes in v1:
time: 334 us; the launch traced here: 329 us
  Pallas kernels  142 us (43%)
  local copies, waits for them, and re-layouts  79.2 us (24%)
  waiting for transfers between devices  48 us (14%)
  starting transfers between devices  21.6 us (6%)
  other arithmetic  20.5 us (6%)
  matrix products  14.4 us (4%)
    pallas_call x1, Pallas kernels, near_call(): pl.pallas_call(functools.partial(near_kernel, ku, slots, own_first), out_...  142 us
    gather x3, local copies, waits for them, and re-layouts, local(): extended_multipoles[rows]  56.3 us
    ppermute x8, waiting for transfers between devices, shifted(): return lax.ppermute(array, axis, pairs)  48 us
    ppermute x8, starting transfers between devices, shifted(): return lax.ppermute(array, axis, pairs)  21.6 us
    another operation x5, local copies, waits for them, and re-layouts, local(): jnp.stack([ext[0], ext[1], ext[2], norm, one, ext[3], zero, zero], axis=1)  17.2 us
    dot_general x1, matrix products, local(): jnp.einsum('bvq,vpq->bp', picked, m2l, precision=lax.Precision.HIGHEST)  13.7 us
    convert_element_type x1, other arithmetic, local(): cnt = ext[4, :, width].astype(jnp.int32)  11.2 us
  transfers between devices with their start and end apart: 8, of which 5 were waited for; matrix products, arithmetic and copies ran while one was open for 2% of the time, Pallas kernels for 0%

profile of v1, /device:TPU:20, one launch (start us, length us, event | category | flops | bytes accessed | tf_op | source)
XLA Modules:
  0.0 328.9 jit_solution(16228857120551375390)
XLA Ops:
  4.7 3.4 %collective-permute-start = (f32[5,64,256]{2,0,1:T(8,128)S(1)}, f32[5,64,256]{2,0,1:T(8,128)}, u32[]{:S(2)}, u32[]{:S(2)}) collective-permute-start(f32[5,64,256]{2,0,1:T(8,128)S(1)} %pad_maximum_fusion), channel_id=1, source_target_pairs={{0,4},{1,5},{2,6},{3,7},{4,8},{5,9},{6,10},{7,11},{8,12},{9,13},{1... | collective-permute-start | bytes 983048 | tf_op jit(solution)/shard_map/ppermute | solution.py:121
  8.1 2.6 collective-permute-start.1
  10.7 3.4 %collective-permute-start.2 = (f32[5,64,256]{2,0,1:T(8,128)S(1)}, f32[5,64,256]{2,0,1:T(8,128)S(1)}, u32[]{:S(2)}, u32[]{:S(2)}) collective-permute-start(f32[5,64,256]{2,0,1:T(8,128)S(1)} %pad_maximum_fusion), channel_id=1, source_target_pairs={{0,2},{1,3},{2,4},{3,5},{4,6},{5,7},{6,8},{7,9},{8,10},{9,11},{10,... | collective-permute-start | bytes 983048 | tf_op jit(solution)/shard_map/ppermute | solution.py:121
  14.1 2.6 collective-permute-start.3
  16.7 3.8 %collective-permute-start.4 = (f32[5,64,256]{2,0,1:T(8,128)S(1)}, f32[5,64,256]{2,0,1:T(8,128)S(1)}, u32[]{:S(2)}, u32[]{:S(2)}) collective-permute-start(f32[5,64,256]{2,0,1:T(8,128)S(1)} %pad_maximum_fusion), channel_id=1, source_target_pairs={{1,0},{2,1},{3,2},{4,3},{5,4},{6,5},{7,6},{8,7},{9,8},{10,9},{11,1... | collective-permute-start | bytes 983048 | tf_op jit(solution)/shard_map/ppermute | solution.py:121
  22.3 2.0 all-gather
  25.1 1.6 compare_convert_fusion
  27.6 16.3 %collective-permute-done = f32[5,64,256]{2,0,1:T(8,128)} collective-permute-done((f32[5,64,256]{2,0,1:T(8,128)S(1)}, f32[5,64,256]{2,0,1:T(8,128)}, u32[]{:S(2)}, u32[]{:S(2)}) %collective-permute-start) | collective-permute-done | bytes 327712 | tf_op jit(solution)/shard_map/ppermute | solution.py:121
  44.0 1.9 collective-permute-start.5
  48.3 1.9 collective-permute-start.6
  50.3 1.9 collective-permute-start.7
  52.6 10.4 %collective-permute-done.5 = f32[5,64,256]{2,0,1:T(8,128)S(1)} collective-permute-done((f32[5,64,256]{2,0,1:T(8,128)S(1)}, f32[5,64,256]{2,0,1:T(8,128)S(1)}, u32[]{:S(2)}, u32[]{:S(2)}) %collective-permute-start.5) | collective-permute-done | bytes 327712 | tf_op jit(solution)/shard_map/ppermute | solution.py:121
  63.0 4.4 %collective-permute-done.6 = f32[5,64,256]{2,0,1:T(8,128)S(1)} collective-permute-done((f32[5,64,256]{2,0,1:T(8,128)S(1)}, f32[5,64,256]{2,0,1:T(8,128)S(1)}, u32[]{:S(2)}, u32[]{:S(2)}) %collective-permute-start.6) | collective-permute-done | bytes 327712 | tf_op jit(solution)/shard_map/ppermute | solution.py:121
  67.4 15.5 %collective-permute-done.7 = f32[5,64,256]{2,0,1:T(8,128)S(1)} collective-permute-done((f32[5,64,256]{2,0,1:T(8,128)S(1)}, f32[5,64,256]{2,0,1:T(8,128)S(1)}, u32[]{:S(2)}, u32[]{:S(2)}) %collective-permute-start.7) | collective-permute-done | bytes 327712 | tf_op jit(solution)/shard_map/ppermute | solution.py:121
  83.0 2.4 slice_bitcast_fusion
  85.3 1.7 fusion.4
  87.1 11.2 %fusion.15.cnt_ref = s32[576]{0:T(1024)S(1)} fusion(f32[5,576,256]{2,0,1:T(8,128)S(1)} %constant_dynamic-update-slice_fusion), kind=kLoop, calls=%fused_computation.15 | loop fusion | flops 576 | bytes 4608 | tf_op jit(solution)/shard_map/convert_element_type | solution.py:163
  101.5 12.1 %stack.11.feat_ref = f32[576,8,256]{2,1,0:T(8,128)} concatenate(f32[576,1,256]{2,1,0:T(1,128)} %get-tuple-element.5, f32[576,1,256]{2,1,0:T(1,128)S(1)} %get-tuple-element.4, f32[576,1,256]{2,1,0:T(1,128)S(1)} %get-tuple-element.3, f32[576,1,256]{2,1,0:T(1,128)} %stack.9, f32[576,1,256]{2,1,0:T(1,128)} %stack_broadcast_in_dim.3, f32[576,1,256]{2,1,0:T(1,128)S(1)} %get-tuple-element.2, ...), dimensions={1} | concatenate | bytes 9437184 | tf_op jit(solution)/shard_map/stack | solution.py:162
  113.6 2.3 copy-done.1
  115.9 142.3 %shard_map.104 = f32[64,1,256]{2,1,0:T(1,128)S(1)} custom-call(s32[1728]{0:T(1024)S(1)} %reshape.19.ids_ref, s32[576]{0:T(1024)S(1)} %fusion.15.cnt_ref, f32[576,8,256]{2,1,0:T(8,128)S(1)} %copy-done.1), custom_call_target="tpu_custom_call" | custom-call | tf_op jit(solution)/shard_map/pallas_call | solution.py:99
  258.8 37.8 %gather_fusion = f32[20224,64]{1,0:T(8,128)} fusion(f32[576,64]{1,0:T(8,128)S(1)} %bitcast.34, s32[20480]{0:T(1024)S(1)} %copy-done.2), kind=kCustom, calls=%fused_computation | custom fusion | bytes 10435584 | tf_op jit(solution)/shard_map/gather | solution.py:170
  296.6 9.0 %copy.35 = f32[20224,64]{0,1:T(8,128)} copy(f32[20224,64]{1,0:T(8,128)} %gather_fusion) | data formatting | bytes 10354688 | tf_op jit(solution)/shard_map/gather | solution.py:170
  305.6 9.5 %reshape.22 = f32[64,316,64]{1,0,2:T(8,128)} reshape(f32[20224,64]{0,1:T(8,128)} %copy.35) | data formatting | bytes 10354688 | tf_op jit(solution)/shard_map/gather | solution.py:170
  315.2 13.7 %fusion.10 = f32[64,64]{1,0:T(8,128)} fusion(f32[316,64,64]{0,2,1:T(8,128)} %param.15, f32[64,316,64]{1,0,2:T(8,128)} %reshape.22, f32[64,316]{1,0:T(8,128)S(1)} %copy-done.3, f32[8,8,64]{2,0,1:T(8,128)S(1)} %fusion.17), kind=kOutput, calls=%fused_computation.8 | convolution fusion | flops 995348480 | bytes 10468352 | tf_op jit(solution)/shard_map/bvq,vpq->bp/dot_general | solution.py:171
  (45 shorter events, 14.2 us)
Async XLA Ops:
  0.6 23.8 %copy-start = (f32[8,64,64]{2,1,0:T(8,128)S(1)}, f32[8,64,64]{2,1,0:T(8,128)}, u32[]{:S(2)}) copy-start(f32[8,64,64]{2,1,0:T(8,128)} %param.14) | copy-start | bytes 393220
  4.7 39.3 %collective-permute-start = (f32[5,64,256]{2,0,1:T(8,128)S(1)}, f32[5,64,256]{2,0,1:T(8,128)}, u32[]{:S(2)}, u32[]{:S(2)}) collective-permute-start(f32[5,64,256]{2,0,1:T(8,128)S(1)} %pad_maximum_fusion), channel_id=1, source_target_pairs={{0,4},{1,5},{2,6},{3,7},{4,8},{5,9},{6,10},{7,11},{8,12},{9,13},{1... | collective-permute-start | bytes 983048 | tf_op jit(solution)/shard_map/ppermute | solution.py:121
  8.1 40.2 %collective-permute-start.1 = (f32[5,64,256]{2,0,1:T(8,128)S(1)}, f32[5,64,256]{2,0,1:T(8,128)S(1)}, u32[]{:S(2)}, u32[]{:S(2)}) collective-permute-start(f32[5,64,256]{2,0,1:T(8,128)S(1)} %pad_maximum_fusion), channel_id=1, source_target_pairs={{0,3},{1,4},{2,5},{3,6},{4,7},{5,8},{6,9},{7,10},{8,11},{9,12},{10... | collective-permute-start | bytes 983048 | tf_op jit(solution)/shard_map/ppermute | solution.py:121
  10.7 39.6 %collective-permute-start.2 = (f32[5,64,256]{2,0,1:T(8,128)S(1)}, f32[5,64,256]{2,0,1:T(8,128)S(1)}, u32[]{:S(2)}, u32[]{:S(2)}) collective-permute-start(f32[5,64,256]{2,0,1:T(8,128)S(1)} %pad_maximum_fusion), channel_id=1, source_target_pairs={{0,2},{1,3},{2,4},{3,5},{4,6},{5,7},{6,8},{7,9},{8,10},{9,11},{10,... | collective-permute-start | bytes 983048 | tf_op jit(solution)/shard_map/ppermute | solution.py:121
  14.1 38.2 %collective-permute-start.3 = (f32[5,64,256]{2,0,1:T(8,128)S(1)}, f32[5,64,256]{2,0,1:T(8,128)S(1)}, u32[]{:S(2)}, u32[]{:S(2)}) collective-permute-start(f32[5,64,256]{2,0,1:T(8,128)S(1)} %pad_maximum_fusion), channel_id=1, source_target_pairs={{0,1},{1,2},{2,3},{3,4},{4,5},{5,6},{6,7},{7,8},{8,9},{9,10},{10,1... | collective-permute-start | bytes 983048 | tf_op jit(solution)/shard_map/ppermute | solution.py:121
  16.7 35.8 %collective-permute-start.4 = (f32[5,64,256]{2,0,1:T(8,128)S(1)}, f32[5,64,256]{2,0,1:T(8,128)S(1)}, u32[]{:S(2)}, u32[]{:S(2)}) collective-permute-start(f32[5,64,256]{2,0,1:T(8,128)S(1)} %pad_maximum_fusion), channel_id=1, source_target_pairs={{1,0},{2,1},{3,2},{4,3},{5,4},{6,5},{7,6},{8,7},{9,8},{10,9},{11,1... | collective-permute-start | bytes 983048 | tf_op jit(solution)/shard_map/ppermute | solution.py:121
  44.0 19.0 %collective-permute-start.5 = (f32[5,64,256]{2,0,1:T(8,128)S(1)}, f32[5,64,256]{2,0,1:T(8,128)S(1)}, u32[]{:S(2)}, u32[]{:S(2)}) collective-permute-start(f32[5,64,256]{2,0,1:T(8,128)S(1)} %pad_maximum_fusion), channel_id=1, source_target_pairs={{2,0},{3,1},{4,2},{5,3},{6,4},{7,5},{8,6},{9,7},{10,8},{11,9},{12,... | collective-permute-start | bytes 983048 | tf_op jit(solution)/shard_map/ppermute | solution.py:121
  48.3 19.1 %collective-permute-start.6 = (f32[5,64,256]{2,0,1:T(8,128)S(1)}, f32[5,64,256]{2,0,1:T(8,128)S(1)}, u32[]{:S(2)}, u32[]{:S(2)}) collective-permute-start(f32[5,64,256]{2,0,1:T(8,128)S(1)} %pad_maximum_fusion), channel_id=1, source_target_pairs={{3,0},{4,1},{5,2},{6,3},{7,4},{8,5},{9,6},{10,7},{11,8},{12,9},{13... | collective-permute-start | bytes 983048 | tf_op jit(solution)/shard_map/ppermute | solution.py:121
  50.3 32.6 %collective-permute-start.7 = (f32[5,64,256]{2,0,1:T(8,128)S(1)}, f32[5,64,256]{2,0,1:T(8,128)S(1)}, u32[]{:S(2)}, u32[]{:S(2)}) collective-permute-start(f32[5,64,256]{2,0,1:T(8,128)S(1)} %pad_maximum_fusion), channel_id=1, source_target_pairs={{4,0},{5,1},{6,2},{7,3},{8,4},{9,5},{10,6},{11,7},{12,8},{13,9},{1... | collective-permute-start | bytes 983048 | tf_op jit(solution)/shard_map/ppermute | solution.py:121
  113.6 2.3 copy-start.1
  115.9 142.9 %copy-start.2 = (s32[20480]{0:T(1024)S(1)}, s32[20480]{0:T(1024)}, u32[]{:S(2)}) copy-start(s32[20480]{0:T(1024)} %pad_clamp_fusion) | copy-start | bytes 245764
  305.6 9.5 %copy-start.3 = (f32[64,316]{1,0:T(8,128)S(1)}, f32[64,316]{1,0:T(8,128)}, u32[]{:S(2)}) copy-start(f32[64,316]{1,0:T(8,128)} %compare_convert_fusion) | copy-start | bytes 242692
